TPU v7x, 512 devices: a whole 4x4x16 slice. The times are simulated.
512 devices in a mesh: lon: 8 (over y, z_hi), mem: 64 (over x, z_lo, core).
Axes of the slice: x: 4, y: 4, z: 16 (z_hi: 2, z_lo: 8; z = z_hi * 8 + z_lo), core: 2. Of those that a mesh axis runs over, the one named last changes fastest.
Arguments:
- ensemble: float32 [64, 98304], P('mem', 'lon')
- increments: bfloat16 [64, 98304], P('mem', 'lon'), may hold values from -6 to 6
- offsets: int32 [192, 7], P('lon'), may hold values from -12 to 12, as said below
- taper: bfloat16 [8, 512, 512], replicated
Outputs:
- covariance_product: float32 [64, 98304], P('mem', 'lon')
Inputs may be any that keep to these rules, and one draw needn't show every extreme that they name: Each row lists 7 different nonzero offsets in ascending order.
All inputs are finite; a program needn't handle non-finite values.
Results may differ from a plain program's by a relative error of at most 0.008.
Values may be sent and summed in bfloat16 or wider, within the bound.
A program may use at most 64 MiB of HBM per device.

v0:
```python
import jax
import jax.numpy as jnp
from jax import lax
from jax.sharding import PartitionSpec as P


def extended_2(block, sides, width):
    for axis, dim in sides:
        count = lax.axis_size(axis)
        forward = [(i, i + 1) for i in range(count - 1)]
        forward.append((count - 1, 0))
        backward = [(target, source) for source, target in forward]
        low = lax.ppermute(
            lax.slice_in_dim(block, block.shape[dim] - width, None, axis=dim), axis, forward
        )
        high = lax.ppermute(lax.slice_in_dim(block, 0, width, axis=dim), axis, backward)
        block = jnp.concatenate([low, block, high], axis=dim)
    return block


def taper_apply(extended, offsets, taper):
    vectors = extended.shape[0]
    block_count = offsets.shape[0]
    block_size = taper.shape[1]
    reach_blocks = block_count // 2
    blocks = extended.reshape(vectors, block_count + 2 * reach_blocks, block_size)
    block_rows = jnp.arange(block_count, dtype=jnp.int32) + reach_blocks
    indices = jnp.concatenate([block_rows[:, None], block_rows[:, None] + offsets], axis=1)
    picked = jnp.take(blocks, indices, axis=1)
    tapered = jnp.einsum("qrsb,sab->qra", picked, taper, preferred_element_type=jnp.float32)
    return tapered.reshape(vectors, block_count * block_size)


def extend_product(factor_one, factor_two, rim_width):
    weighted = (factor_one.astype(jnp.float32) * factor_two.astype(jnp.float32)).astype(
        jnp.bfloat16
    )
    return extended_2(weighted, (("lon", 1),), rim_width)


def on_device(ensemble, increments, offsets, taper):
    member_count = lax.axis_size("mem") * ensemble.shape[0]
    rim_width = offsets.shape[0] // 2 * taper.shape[1]
    ens_mean = lax.psum(jnp.sum(ensemble, axis=0), "mem") / member_count
    perturb = (ensemble - ens_mean[None, :]).astype(jnp.bfloat16)
    increments_all = lax.all_gather(increments, "mem", axis=0, tiled=True)
    extended = extend_product(perturb, increments_all, rim_width)
    tapered = taper_apply(extended, offsets, taper)
    summed = lax.psum_scatter(
        perturb.astype(jnp.float32) * tapered, "mem", scatter_dimension=0, tiled=True
    )
    return summed / (member_count - 1)


def solution(mesh):
    return jax.shard_map(
        on_device,
        mesh=mesh,
        in_specs=(P("mem", "lon"), P("mem", "lon"), P("lon", None), P()),
        out_specs=P("mem", "lon"),
        check_vma=False,
    )
```

profile of v0, /device:TPU:1, one launch (start us, length us, event | category | flops | bytes accessed | tf_op | source)
XLA Modules:
  0.0 1426.9 jit_solution(17073919097878806883)
XLA Ops:
  6.5 0.0 all-gather.3.cloned.1.call-start
  6.5 0.7 all-gather.3.cloned.1.call-update
  7.3 0.0 all-reduce.3.cloned.1.call-start
  7.3 504.5 %psum.7 = f32[12288]{0:T(1024)S(1)} all-reduce(f32[12288]{0:T(1024)} %bitcast.42), channel_id=1, replica_groups=mesh['lon'=8,'mem'=64] {'mem'}, use_global_device_ids=true, to_apply=%region_0.0 | all-reduce | flops 12288 | bytes 98304 | tf_op jit(solution)/shard_map/psum | solution.py:44
  511.9 0.8 convert_convert_fusion
  512.7 0.0 all-gather.3.cloned.1.call-done
  512.7 0.0 copy-start
  512.7 3.6 fusion.6
  516.4 1.3 fusion.14
  517.7 7.0 collective-permute-start
  524.7 9.1 collective-permute-start.1
  533.8 0.0 copy-done
  533.9 0.1 copy.22
  533.9 0.1 reshape.98
  534.1 0.1 copy.19
  534.2 15.4 %collective-permute-done = bf16[64,6144]{1,0:T(8,128)(2,1)S(1)} collective-permute-done((bf16[64,6144]{1,0:T(8,128)(2,1)}, bf16[64,6144]{1,0:T(8,128)(2,1)S(1)}, u32[]{:S(2)}, u32[]{:S(2)}) %collective-permute-start) | collective-permute-done | bytes 786464 | tf_op jit(solution)/shard_map/ppermute | solution.py:13
  549.6 15.8 %collective-permute-done.1 = bf16[64,6144]{1,0:T(8,128)(2,1)S(1)} collective-permute-done((bf16[64,6144]{1,0:T(8,128)(2,1)}, bf16[64,6144]{1,0:T(8,128)(2,1)S(1)}, u32[]{:S(2)}, u32[]{:S(2)}) %collective-permute-start.1) | collective-permute-done | bytes 786464 | tf_op jit(solution)/shard_map/ppermute | solution.py:16
  565.4 0.2 pad_maximum_fusion
  565.6 0.4 copy.30
  566.0 8.2 gather_fusion
  574.2 10.6 fusion.7
  584.9 0.3 copy.27
  585.2 1.9 broadcast_multiply_fusion
  587.1 0.0 all-reduce.3.cloned.1.call-update
  587.2 1.3 dynamic-slice
  588.5 829.2 %all-reduce.3.cloned.1.call-done = f32[64,12288]{1,0:T(8,128)} async-done(((f32[64,12288]{1,0:T(8,128)}), f32[64,12288]{1,0:T(8,128)}) %all-reduce.3.cloned.1.call-update) | async-done | bytes 3145744
  1417.7 2.4 dynamic-slice_multiply_fusion
  (9 shorter events, 0.1 us)
Async XLA Ops:
  6.5 506.2 %all-gather.3.cloned.1.call-start = ((), (), s32[]{:S(2)}) async-start(), calls=%async_computation | async-start | bytes 3194880 | tf_op jit(solution)/shard_map/all_gather | solution.py:46
  7.3 1410.4 %all-reduce.3.cloned.1.call-start = ((), (), s32[]{:S(2)}) async-start(), calls=%async_computation.1 | async-start | bytes 6291456
  512.7 21.1 %copy-start = (s32[24,7]{0,1:T(8,128)S(1)}, s32[24,7]{0,1:T(8,128)}, u32[]{:S(2)}) copy-start(s32[24,7]{0,1:T(8,128)} %param.6) | copy-start | bytes 2020
  517.7 31.9 %collective-permute-start = (bf16[64,6144]{1,0:T(8,128)(2,1)}, bf16[64,6144]{1,0:T(8,128)(2,1)S(1)}, u32[]{:S(2)}, u32[]{:S(2)}) collective-permute-start(bf16[64,6144]{1,0:T(8,128)(2,1)} %get-tuple-element.5), channel_id=1, source_target_pairs={{0,64},{64,128},{128,192},{192,256},{256,320},{320,384},{384,448},... | collective-permute-start | bytes 2359304 | tf_op jit(solution)/shard_map/ppermute | solution.py:13
  524.7 40.6 %collective-permute-start.1 = (bf16[64,6144]{1,0:T(8,128)(2,1)}, bf16[64,6144]{1,0:T(8,128)(2,1)S(1)}, u32[]{:S(2)}, u32[]{:S(2)}) collective-permute-start(bf16[64,6144]{1,0:T(8,128)(2,1)} %get-tuple-element.6), channel_id=1, source_target_pairs={{64,0},{128,64},{192,128},{256,192},{320,256},{384,320},{448,384},... | collective-permute-start | bytes 2359304 | tf_op jit(solution)/shard_map/ppermute | solution.py:16
Sparse Core Ops, SparseCore 0:
  9.5 127.7 all-gather.2
  587.3 830.3 all-reduce.2
where the time goes:
time: 1430 us
  waiting for transfers between devices  861 us (60%)
  blocking collectives  505 us (35%)
  starting transfers between devices  16.1 us (1%)
    unnamed x3, waiting for transfers between devices  830 us
    psum x1, blocking collectives, on_device(): ens_mean = lax.psum(jnp.sum(ensemble, axis=0), 'mem') / member_count  505 us
  transfers between devices with their start and end apart: 4, of which 3 were waited for; matrix products, arithmetic and copies ran while one was open for 0% of the time, Pallas kernels for 0%

commit v1 on v0

--- a/solution.py
+++ b/solution.py
@@ -2,6 +2,11 @@
 import jax.numpy as jnp
 from jax import lax
 from jax.sharding import PartitionSpec as P
+
+
+def add_all(shard, axis):
+    shards = lax.all_gather(shard, axis)
+    return jnp.sum(shards, axis=0)
 
 
 def extended_2(block, sides, width):
@@ -41,7 +46,7 @@
 def on_device(ensemble, increments, offsets, taper):
     member_count = lax.axis_size("mem") * ensemble.shape[0]
     rim_width = offsets.shape[0] // 2 * taper.shape[1]
-    ens_mean = lax.psum(jnp.sum(ensemble, axis=0), "mem") / member_count
+    ens_mean = add_all(jnp.sum(ensemble, axis=0), "mem") / member_count
     perturb = (ensemble - ens_mean[None, :]).astype(jnp.bfloat16)
     increments_all = lax.all_gather(increments, "mem", axis=0, tiled=True)
     extended = extend_product(perturb, increments_all, rim_width)

time: 1430 us -> 1280 us (0.90)
  blocking collectives: 505 us -> 0 us
  waiting for transfers between devices: 861 us -> 1210 us
    psum x1 -> x0, blocking collectives: 505 us -> none  [on_device(): ens_mean = lax.psum(jnp.sum(ensemble, axis=0), 'mem') / member_count]
    all_gather x0 -> x1, waiting for transfers between devices: none -> 129 us  [add_all(): shards = lax.all_gather(shard, axis)]
    all_gather x1, waiting for transfers between devices: 0.02 us -> 115 us  [on_device(): increments_all = lax.all_gather(increments, 'mem', axis=0, tiled=True)]
    unnamed x3 -> x4, waiting for transfers between devices: 830 us -> 881 us
    ppermute x1, waiting for transfers between devices: 15.8 us -> 51.3 us  [extended_2(): lax.ppermute(lax.slice_in_dim(block, 0, width, axis=dim), axis, backward)]
    ppermute x1, waiting for transfers between devices: 15.4 us -> 34.6 us  [extended_2(): lax.ppermute(lax.slice_in_dim(block, block.shape[dim] - width, None, axis...]
  transfers between devices with their start and end apart: 4 -> 5, of which waited for: 3 -> 5; matrix products, arithmetic and copies ran while one was open for 0% -> 0% of each run, Pallas kernels for 0% -> 0%
where the time goes in v1:
time: 1280 us
  waiting for transfers between devices  1210 us (95%)
  starting transfers between devices  16.2 us (1%)
  between operations  13.2 us (1%)
  other arithmetic  12.8 us (1%)
    unnamed x4, waiting for transfers between devices  881 us
    all_gather x1, waiting for transfers between devices, add_all(): shards = lax.all_gather(shard, axis)  129 us
    all_gather x1, waiting for transfers between devices, on_device(): increments_all = lax.all_gather(increments, 'mem', axis=0, tiled=True)  115 us
    ppermute x1, waiting for transfers between devices, extended_2(): lax.ppermute(lax.slice_in_dim(block, 0, width, axis=dim), axis, backward)  51.3 us
    ppermute x1, waiting for transfers between devices, extended_2(): lax.ppermute(lax.slice_in_dim(block, block.shape[dim] - width, None, axis...  34.6 us
  transfers between devices with their start and end apart: 5, of which 5 were waited for; matrix products, arithmetic and copies ran while one was open for 0% of the time, Pallas kernels for 0%

profile of v1, /device:TPU:1, one launch (start us, length us, event | category | flops | bytes accessed | tf_op | source)
XLA Modules:
  0.0 1275.7 jit_solution(4548390809056572525)
XLA Ops:
  6.5 0.0 copy-start
  6.5 0.0 all-gather.5.cloned.1.call-start
  6.5 0.7 all-gather.5.cloned.1.call-update
  7.3 0.0 all-gather.7.cloned.1.call-start
  7.3 0.7 all-gather.7.cloned.1.call-update
  8.0 0.0 all-reduce.3.cloned.1.call-start
  8.1 129.3 %all-gather.5.cloned.1.call-done = f32[64,1,12288]{2,1,0:T(1,128)} async-done(((f32[1,1,12288]{2,1,0:T(1,128)}), f32[64,1,12288]{2,1,0:T(1,128)}) %all-gather.5.cloned.1.call-update) | async-done | bytes 3145744 | tf_op jit(solution)/shard_map/all_gather | solution.py:8
  137.4 4.5 reduce_sum.8
  142.0 0.0 copy-done
  142.0 0.1 convert_convert_fusion
  142.0 115.1 %all-gather.7.cloned.1.call-done = bf16[64,1,12288]{2,1,0:T(2,128)(2,1)} async-done(((bf16[1,1,12288]{2,1,0:T(2,128)(2,1)}), bf16[64,1,12288]{2,1,0:T(2,128)(2,1)}) %all-gather.7.cloned.1.call-update) | async-done | bytes 1572880 | tf_op jit(solution)/shard_map/all_gather | solution.py:51
  257.2 0.0 copy-start.1
  257.2 3.6 fusion.6
  260.8 1.3 fusion.14
  262.1 8.4 collective-permute-start
  270.4 7.7 collective-permute-start.1
  278.2 0.0 copy-done.1
  278.2 0.1 copy.22
  278.3 0.1 reshape.108
  278.4 0.1 copy.19
  278.5 34.6 %collective-permute-done = bf16[64,6144]{1,0:T(8,128)(2,1)S(1)} collective-permute-done((bf16[64,6144]{1,0:T(8,128)(2,1)}, bf16[64,6144]{1,0:T(8,128)(2,1)S(1)}, u32[]{:S(2)}, u32[]{:S(2)}) %collective-permute-start) | collective-permute-done | bytes 786464 | tf_op jit(solution)/shard_map/ppermute | solution.py:18
  313.1 51.3 %collective-permute-done.1 = bf16[64,6144]{1,0:T(8,128)(2,1)S(1)} collective-permute-done((bf16[64,6144]{1,0:T(8,128)(2,1)}, bf16[64,6144]{1,0:T(8,128)(2,1)S(1)}, u32[]{:S(2)}, u32[]{:S(2)}) %collective-permute-start.1) | collective-permute-done | bytes 786464 | tf_op jit(solution)/shard_map/ppermute | solution.py:21
  364.4 0.2 pad_maximum_fusion
  364.7 0.4 copy.30
  365.0 8.2 gather_fusion
  373.2 10.6 fusion.7
  383.9 0.3 copy.27
  384.2 1.9 broadcast_multiply_fusion
  386.1 0.0 all-reduce.3.cloned.1.call-update
  386.2 1.3 dynamic-slice
  387.5 879.4 %all-reduce.3.cloned.1.call-done = f32[64,12288]{1,0:T(8,128)} async-done(((f32[64,12288]{1,0:T(8,128)}), f32[64,12288]{1,0:T(8,128)}) %all-reduce.3.cloned.1.call-update) | async-done | bytes 3145744
  1266.9 2.3 dynamic-slice_multiply_fusion
  (9 shorter events, 0.1 us)
Async XLA Ops:
  6.5 135.4 %copy-start = (f32[1,12288]{1,0:T(1,128)S(1)}, f32[1,12288]{1,0:T(1,128)}, u32[]{:S(2)}) copy-start(f32[1,12288]{1,0:T(1,128)} %param.4) | copy-start | bytes 147460
  6.5 130.9 %all-gather.5.cloned.1.call-start = ((), (), s32[]{:S(2)}) async-start(), calls=%async_computation | async-start | bytes 3194880 | tf_op jit(solution)/shard_map/all_gather | solution.py:8
  7.3 249.9 %all-gather.7.cloned.1.call-start = ((), (), s32[]{:S(2)}) async-start(), calls=%async_computation.1 | async-start | bytes 3194880 | tf_op jit(solution)/shard_map/all_gather | solution.py:51
  8.0 1258.9 %all-reduce.3.cloned.1.call-start = ((), (), s32[]{:S(2)}) async-start(), calls=%async_computation.2 | async-start | bytes 6291456
  257.2 21.0 %copy-start.1 = (s32[24,7]{0,1:T(8,128)S(1)}, s32[24,7]{0,1:T(8,128)}, u32[]{:S(2)}) copy-start(s32[24,7]{0,1:T(8,128)} %param.6) | copy-start | bytes 2020
  262.1 51.1 %collective-permute-start = (bf16[64,6144]{1,0:T(8,128)(2,1)}, bf16[64,6144]{1,0:T(8,128)(2,1)S(1)}, u32[]{:S(2)}, u32[]{:S(2)}) collective-permute-start(bf16[64,6144]{1,0:T(8,128)(2,1)} %get-tuple-element.5), channel_id=1, source_target_pairs={{0,64},{64,128},{128,192},{192,256},{256,320},{320,384},{384,448},... | collective-permute-start | bytes 2359304 | tf_op jit(solution)/shard_map/ppermute | solution.py:18
  270.4 94.0 %collective-permute-start.1 = (bf16[64,6144]{1,0:T(8,128)(2,1)}, bf16[64,6144]{1,0:T(8,128)(2,1)S(1)}, u32[]{:S(2)}, u32[]{:S(2)}) collective-permute-start(bf16[64,6144]{1,0:T(8,128)(2,1)} %get-tuple-element.6), channel_id=1, source_target_pairs={{64,0},{128,64},{192,128},{256,192},{320,256},{384,320},{448,384},... | collective-permute-start | bytes 2359304 | tf_op jit(solution)/shard_map/ppermute | solution.py:21
Sparse Core Ops, SparseCore 0:
  9.5 127.8 all-gather.4
  139.5 117.5 all-gather.6
  386.3 880.5 all-reduce.2
